TPU v7x, 32 devices: a whole 2x2x4 slice. The times are simulated.
32 devices in a mesh: groups: 2 (over x), dp: 8 (over z, y), narrow: 2 (over core).
Axes of the slice: x: 2, y: 2, z: 4, core: 2. Of those that a mesh axis runs over, the one named last changes fastest.
Arguments:
- tokens: bfloat16 [12288, 8192], P(('groups', 'dp'), 'narrow'), parts along dimension 0, may hold values from -6 to 6
- req_adapter: int32 [96], P(('groups', 'dp')), parts along dimension 0, may hold values from 0 to 15
- value_weight: bfloat16 [8192, 1024], P('narrow'), may hold values from -0.0625 to 0.0625
- adapter_down: bfloat16 [16, 64, 8192], P(None, 'dp', 'narrow'), may hold values from -0.0625 to 0.0625
- adapter_up: bfloat16 [16, 64, 1024], P(None, 'dp', 'narrow'), may hold values from -0.75 to 0.75
Outputs:
- values_out: bfloat16 [12288, 1024], P(('groups', 'dp'), 'narrow'), parts along dimension 0
There are 2 independent parts, one for each index of `groups`. A program takes and returns all parts, laid end to end along the dimension named above; an argument that names none is the same for every part. Nothing has to cross between parts.
All inputs are finite; a program needn't handle non-finite values.
Results may differ from a plain program's by a relative error of at most 0.0053.
Values may be sent and summed in bfloat16 or wider, within the bound.
A program may use at most 128 MiB of HBM per device.

v0:
```python
import jax
import jax.numpy as jnp
from jax import lax
from jax.sharding import PartitionSpec as P


def per_device(tokens, req_adapter, value_weight, adapter_down, adapter_up):
    partial_base = jnp.dot(tokens, value_weight, preferred_element_type=jnp.float32)
    base = lax.psum_scatter(partial_base, "narrow", scatter_dimension=1, tiled=True)
    tok_count = tokens.shape[0]
    half_width = tokens.shape[1]
    req_count = req_adapter.shape[0]
    req_len = tok_count // req_count
    col_count = adapter_up.shape[2]
    blocks = tokens.reshape(req_count, req_len, half_width)
    chosen = jnp.take(lax.all_gather(adapter_down, "dp", axis=1, tiled=True), req_adapter, axis=0)
    result = jnp.einsum("qtd,qrd->qtr", blocks, chosen, preferred_element_type=jnp.float32)
    shrunk = lax.psum(result, "narrow").astype(jnp.bfloat16)
    chosen = jnp.take(lax.all_gather(adapter_up, "dp", axis=1, tiled=True), req_adapter, axis=0)
    delta = jnp.einsum("qtr,qrc->qtc", shrunk, chosen, preferred_element_type=jnp.float32)
    delta = delta.astype(jnp.bfloat16).reshape(tok_count, col_count)
    return (base + delta.astype(jnp.float32)).astype(jnp.bfloat16)


def solution(mesh):
    in_specs = (
        P(("groups", "dp"), "narrow"),
        P(("groups", "dp")),
        P("narrow", None),
        P(None, "dp", "narrow"),
        P(None, "dp", "narrow"),
    )
    out_specs = P(("groups", "dp"), "narrow")
    return jax.shard_map(
        per_device, mesh=mesh, in_specs=in_specs, out_specs=out_specs, check_vma=False
    )
```

profile of v0, /device:TPU:0, one launch (start us, length us, event | category | flops | bytes accessed | tf_op | source)
XLA Modules:
  0.0 204.0 jit_solution(13067462054842741423)
XLA Ops:
  7.4 0.0 all-gather.5.cloned.1.call-start
  7.4 0.7 all-gather.5.cloned.1.call-update
  8.1 0.0 all-gather.3.cloned.1.call-start
  8.1 0.7 all-gather.3.cloned.1.call-update
  8.8 0.0 reduce-scatter.2.cloned.1.call-start
  8.9 12.1 %fusion.14 = f32[768,1024]{1,0:T(8,128)} fusion(bf16[768,4096]{1,0:T(8,128)(2,1)} %param.5, bf16[4096,1024]{1,0:T(8,128)(2,1)} %param.7), kind=kOutput, calls=%fused_computation.19 | convolution fusion | flops 6442450944 | bytes 17825792 | tf_op jit(solution)/shard_map/dot_general | solution.py:8
  20.9 0.0 copy-start
  20.9 0.0 reduce-scatter.2.cloned.1.call-update
  21.0 0.6 copy-done
  21.6 31.1 %all-gather.5.cloned.1.call-done = bf16[16,64,512]{2,1,0:T(8,128)(2,1)} async-done(((bf16[16,8,512]{2,1,0:T(8,128)(2,1)}), bf16[16,64,512]{2,1,0:T(8,128)(2,1)}) %all-gather.5.cloned.1.call-update) | async-done | bytes 1048592 | tf_op jit(solution)/shard_map/all_gather | solution.py:19
  52.7 1.8 gather_fusion.1
  54.5 124.4 %all-gather.3.cloned.1.call-done = bf16[16,64,4096]{2,1,0:T(8,128)(2,1)} async-done(((bf16[16,8,4096]{2,1,0:T(8,128)(2,1)}), bf16[16,64,4096]{2,1,0:T(8,128)(2,1)}) %all-gather.3.cloned.1.call-update) | async-done | bytes 8388624 | tf_op jit(solution)/shard_map/all_gather | solution.py:16
  178.9 4.1 %gather_fusion = bf16[6,64,4096]{2,1,0:T(8,128)(2,1)S(1)} fusion(bf16[16,64,4096]{2,1,0:T(8,128)(2,1)} %all-gather.3.cloned.1.call-done, s32[1024]{0:T(1024)S(1)} %pad_clamp_fusion), kind=kCustom, calls=%fused_computation | custom fusion | bytes 6291480 | tf_op jit(solution)/shard_map/jit(_take)/gather | solution.py:16
  183.1 5.8 %fusion.5 = f32[6,128,64]{1,2,0:T(8,128)} fusion(bf16[6,128,4096]{2,1,0:T(8,128)(2,1)} %bitcast.10, bf16[6,64,4096]{2,1,0:T(8,128)(2,1)S(1)} %gather_fusion, pred[6]{0:T(512)(128)(4,1)S(1)} %compare_and_fusion), kind=kOutput, calls=%fused_computation.9 | convolution fusion | flops 404226048 | bytes 9633798 | tf_op jit(solution)/shard_map/qtd,qrd->qtr/dot_general | solution.py:17
  188.9 4.7 %all-reduce.1 = bf16[6,128,64]{1,2,0:T(8,128)(2,1)S(1)} all-reduce(f32[6,128,64]{1,2,0:T(8,128)} %fusion.5), channel_id=1, replica_groups=mesh['groups'=2,'dp'=8,'narrow'=2] {'narrow'}, use_global_device_ids=true, to_apply=%region_1.2 | all-reduce | flops 49152 | bytes 294912 | tf_op jit(solution)/shard_map/psum | solution.py:18
  193.6 0.4 convolution_convert_fusion
  194.0 0.0 reduce-scatter.2.cloned.1.call-done
  194.1 2.5 %fusion.3 = bf16[768,512]{1,0:T(8,128)(2,1)} fusion(f32[768,512]{1,0:T(8,128)} %reduce-scatter.2.cloned.1.call-done, bf16[6,128,512]{2,1,0:T(8,128)(2,1)S(1)} %convolution_convert_fusion), kind=kLoop, calls=%fused_computation.6 | loop fusion | flops 1179648 | bytes 3145728 | tf_op jit(solution)/shard_map/convert_element_type | solution.py:22
  (3 shorter events, 0.0 us)
Async XLA Ops:
  7.4 45.3 %all-gather.5.cloned.1.call-start = ((), (), s32[]{:S(2)}) async-start(), calls=%async_computation.3 | async-start | bytes 1179648 | tf_op jit(solution)/shard_map/all_gather | solution.py:19
  8.1 170.9 %all-gather.3.cloned.1.call-start = ((), (), s32[]{:S(2)}) async-start(), calls=%async_computation.2 | async-start | bytes 9437184 | tf_op jit(solution)/shard_map/all_gather | solution.py:16
  8.8 185.2 %reduce-scatter.2.cloned.1.call-start = ((), (), s32[]{:S(2)}) async-start(), calls=%async_computation.1 | async-start | bytes 4718592 | tf_op jit(solution)/shard_map/reduce_scatter | solution.py:9
  20.9 0.7 copy-start
Sparse Core Ops, SparseCore 0:
  10.4 42.2 all-gather.4
  55.1 123.7 all-gather.2
Sparse Core Ops, SparseCore 1:
  21.1 13.4 reduce-scatter.1
where the time goes:
time: 204 us
  waiting for transfers between devices  157 us (77%)
  matrix products  18.3 us (9%)
  between operations  14.9 us (7%)
  local copies, waits for them, and re-layouts  6.55 us (3%)
  blocking collectives  4.69 us (2%)
  other arithmetic  2.56 us (1%)
    all_gather x1, waiting for transfers between devices, per_device(): lax.all_gather(adapter_down, 'dp', axis=1, tiled=True)  124 us
    all_gather x1, waiting for transfers between devices, per_device(): lax.all_gather(adapter_up, 'dp', axis=1, tiled=True)  31.1 us
    dot_general x1, matrix products, per_device(): jnp.dot(tokens, value_weight, preferred_element_type=jnp.float32)  12.1 us
    dot_general x1, matrix products, per_device(): jnp.einsum('qtd,qrd->qtr', blocks, chosen, preferred_element_type=jnp.flo...  5.81 us
    psum x1, blocking collectives, per_device(): shrunk = lax.psum(result, 'narrow').astype(jnp.bfloat16)  4.69 us
    gather x1, local copies, waits for them, and re-layouts, per_device(): jnp.take(lax.all_gather(adapter_down, 'dp', axis=1, tiled=True), req_adap...  4.13 us
  transfers between devices with their start and end apart: 3, of which 2 were waited for; matrix products, arithmetic and copies ran while one was open for 12% of the time, Pallas kernels for 0%

commit v1 on v0

--- a/solution.py
+++ b/solution.py
@@ -1,10 +1,17 @@
 import jax
 import jax.numpy as jnp
 from jax import lax
+from jax.experimental import pallas as pl
+from jax.experimental.pallas import tpu as pltpu
 from jax.sharding import PartitionSpec as P
 
-
-def per_device(tokens, req_adapter, value_weight, adapter_down, adapter_up):
+MESH = pl.DeviceIdType.MESH
+PLANES = 4
+CHUNKS = 2
+TILE = 256
+
+
+def gathered(tokens, req_adapter, value_weight, adapter_down, adapter_up):
     partial_base = jnp.dot(tokens, value_weight, preferred_element_type=jnp.float32)
     base = lax.psum_scatter(partial_base, "narrow", scatter_dimension=1, tiled=True)
     tok_count = tokens.shape[0]
@@ -22,6 +29,302 @@
     return (base + delta.astype(jnp.float32)).astype(jnp.bfloat16)
 
 
+def kernel(
+    req_ref, tok_hbm, w_hbm, down_hbm, up_hbm, out_ref,
+    tok, w, slots, pack, recv, ids_v, ids_s, peer_base, got_base, own_base, part, got_part,
+    load_sem, zload_sem, idload_sem, z_send, z_recv, p_send, p_recv, id_send, id_recv,
+    base_send, base_recv, part_send, part_recv,
+):
+    g, d, c = lax.axis_index("groups"), lax.axis_index("dp"), lax.axis_index("narrow")
+    z, y = d // 2, d % 2
+    requests = recv.shape[1]
+    rows = tok.shape[0] // requests
+    rank = down_hbm.shape[1]
+    dhalf = down_hbm.shape[2] // 2
+    uhalf = up_hbm.shape[2] // 2
+    wide = recv.shape[-1]
+
+    def slot(way, step, chunk):
+        return slots[chunk * (2 * PLANES - 1) + (0 if step < 0 else 1 + way * (PLANES - 1) + step)]
+
+    cols = out_ref.shape[1]
+    above, below = (g, d + 2, c), (g, d - 2, c)
+    yflip = d + 1 - 2 * y
+    around = ((1 - g, d, c), (g, yflip, c), (1 - g, yflip, c))
+    other = (g, d, 1 - c)
+
+    zloads = []
+    for chunk in range(CHUNKS):
+        low, high = chunk * wide, (chunk + 1) * wide
+        pieces = []
+        if low < dhalf:
+            size = min(high, dhalf) - low
+            src = pl.ds(pl.multiple_of(g * dhalf + low, 128), size)
+            pieces.append((down_hbm.at[:, :, src], slot(0, -1, chunk).at[:, :, pl.ds(0, size)]))
+        if high > dhalf:
+            start = max(low, dhalf)
+            size = high - start
+            src = pl.ds(pl.multiple_of(g * uhalf + start - dhalf, 128), size)
+            pieces.append((up_hbm.at[:, :, src], slot(0, -1, chunk).at[:, :, pl.ds(start - low, size)]))
+        for place, (src, dst) in enumerate(pieces):
+            copy = pltpu.make_async_copy(src, dst, zload_sem.at[chunk, place])
+            copy.start()
+            zloads.append((chunk, copy))
+    tok_load = pltpu.make_async_copy(tok_hbm, tok, load_sem.at[0])
+    w_load = pltpu.make_async_copy(w_hbm, w, load_sem.at[1])
+    tok_load.start()
+    w_load.start()
+
+    lane = lax.broadcasted_iota(jnp.int32, ids_v.shape[1:], 1)
+    ids = jnp.zeros(ids_v.shape[1:], jnp.int32)
+    for q in range(requests):
+        ids = jnp.where(lane == q, req_ref[q], ids)
+    ids_v[3] = ids
+
+    barrier = pltpu.get_barrier_semaphore()
+    for target in around + (other,):
+        pl.semaphore_signal(barrier, inc=1, device_id=target, device_id_type=MESH)
+
+    @pl.when(z < PLANES - 1)
+    def _():
+        pl.semaphore_signal(barrier, inc=1, device_id=above, device_id_type=MESH)
+
+    @pl.when(z > 0)
+    def _():
+        pl.semaphore_signal(barrier, inc=1, device_id=below, device_id_type=MESH)
+
+    pl.semaphore_wait(barrier, 4 + (z + PLANES - 1) // PLANES + (2 * PLANES - 2 - z) // PLANES)
+
+    def z_copy(way, step, chunk):
+        return pltpu.make_async_remote_copy(
+            src_ref=slot(way, step - 1, chunk), dst_ref=slot(way, step, chunk),
+            send_sem=z_send.at[way, step, chunk], recv_sem=z_recv.at[way, step, chunk],
+            device_id=above if way == 0 else below, device_id_type=MESH,
+        )
+
+    def z_sends(way, step):
+        return z - step >= 0 if way == 0 else z + step <= PLANES - 1
+
+    def z_can(way, step):
+        if way == 0:
+            return jnp.logical_and(z < PLANES - 1, z_sends(way, step))
+        return jnp.logical_and(z > 0, z_sends(way, step))
+
+    def z_arrives(way, step):
+        return z - 1 - step >= 0 if way == 0 else z + 1 + step <= PLANES - 1
+
+    def p_copy(block, relation, chunk):
+        return pltpu.make_async_remote_copy(
+            src_ref=pack.at[chunk, block, relation],
+            dst_ref=recv.at[chunk, :, g, block, y],
+            send_sem=p_send.at[chunk, block, relation], recv_sem=p_recv.at[chunk, block, relation],
+            device_id=around[relation], device_id_type=MESH,
+        )
+
+    def p_arrival(block, relation, chunk):
+        from_g = g if relation == 1 else 1 - g
+        from_y = y if relation == 0 else 1 - y
+        return pltpu.make_async_remote_copy(
+            src_ref=pack.at[chunk, block, relation],
+            dst_ref=recv.at[chunk, :, from_g, block, from_y],
+            send_sem=p_send.at[chunk, block, relation], recv_sem=p_recv.at[chunk, block, relation],
+            device_id=around[relation], device_id_type=MESH,
+        )
+
+    def share(way, step, chunk):
+        held = slot(way, step, chunk)
+        block = z - 1 - step if way == 0 else z + 1 + step
+        for relation in (2, 0, 1):
+            for q in range(requests):
+                pack[chunk, block, relation, q] = held[ids_s[relation, 0, q]]
+            p_copy(block, relation, chunk).start()
+        for q in range(requests):
+            recv[chunk, q, g, block, y] = held[req_ref[q]]
+
+    def id_copy(relation):
+        return pltpu.make_async_remote_copy(
+            src_ref=ids_v.at[3], dst_ref=ids_v.at[relation],
+            send_sem=id_send.at[relation], recv_sem=id_recv.at[relation],
+            device_id=around[relation], device_id_type=MESH,
+        )
+
+    for relation in range(3):
+        id_copy(relation).start()
+    for chunk in range(CHUNKS):
+        for which, copy in zloads:
+            if which == chunk:
+                copy.wait()
+        for way in range(2):
+            @pl.when(z_can(way, 0))
+            def _():
+                z_copy(way, 0, chunk).start()
+
+    for relation in range(3):
+        id_copy(relation).wait()
+        id_load = pltpu.make_async_copy(ids_v.at[relation], ids_s.at[relation], idload_sem.at[relation])
+        id_load.start()
+        id_load.wait()
+    for chunk in range(CHUNKS):
+        share(0, -1, chunk)
+
+    tok_load.wait()
+    w_load.wait()
+
+    m_tiles = tok.shape[0] // TILE
+    n_tiles = cols // TILE
+
+    def base(first, dst, low, high):
+        def tile(i, _):
+            n, m = i // m_tiles, i % m_tiles
+            at = pl.ds(pl.multiple_of(m * TILE, TILE), TILE)
+            dst[at, pl.ds(pl.multiple_of(n * TILE, TILE), TILE)] = jnp.dot(
+                tok[at, :], w[:, pl.ds(pl.multiple_of(first + n * TILE, TILE), TILE)],
+                preferred_element_type=jnp.float32,
+            )
+            return 0
+
+        lax.fori_loop(low, high, tile, 0)
+
+    base_copy = pltpu.make_async_remote_copy(
+        src_ref=peer_base, dst_ref=got_base, send_sem=base_send, recv_sem=base_recv,
+        device_id=other, device_id_type=MESH,
+    )
+    tiles = m_tiles * n_tiles
+
+    def pass_on(step, chunk):
+        for way in range(2):
+            @pl.when(z_arrives(way, step))
+            def _():
+                z_copy(way, step, chunk).wait_recv()
+        if step + 1 < PLANES - 1:
+            for way in range(2):
+                @pl.when(z_can(way, step + 1))
+                def _():
+                    z_copy(way, step + 1, chunk).start()
+        for way in range(2):
+            @pl.when(z_arrives(way, step))
+            def _():
+                share(way, step, chunk)
+
+    base((1 - c) * cols, peer_base, 0, tiles)
+    base_copy.start()
+    pass_on(0, 0)
+    base(c * cols, own_base, 0, tiles // 2)
+    pass_on(0, 1)
+    base(c * cols, own_base, tiles // 2, tiles)
+    for step in range(1, PLANES - 1):
+        for chunk in range(CHUNKS):
+            pass_on(step, chunk)
+
+    for chunk in range(CHUNKS):
+        for block in range(PLANES):
+            for relation in range(3):
+                p_arrival(block, relation, chunk).wait_recv()
+
+    full = PLANES * 2 * rank
+
+    def picked(q, side, chunk):
+        rows8 = recv[chunk, q, side].astype(jnp.float32)
+        return rows8.reshape(full, wide).astype(jnp.bfloat16)
+
+    def part_copy(q):
+        return pltpu.make_async_remote_copy(
+            src_ref=part.at[q], dst_ref=got_part.at[q],
+            send_sem=part_send.at[q], recv_sem=part_recv.at[q],
+            device_id=other, device_id_type=MESH,
+        )
+
+    for q in range(requests):
+        at = pl.ds(q * rows, rows)
+        total = jnp.zeros((rows, full), jnp.float32)
+        for side in range(2):
+            for chunk in range(CHUNKS):
+                low = chunk * wide
+                size = min(low + wide, dhalf) - low
+                if size > 0:
+                    total += lax.dot_general(
+                        tok[at, pl.ds(side * dhalf + low, size)], picked(q, side, chunk)[:, :size],
+                        (((1,), (1,)), ((), ())), preferred_element_type=jnp.float32,
+                    )
+        part[q] = total
+        part_copy(q).start()
+
+    base_copy.wait()
+    for q in range(requests):
+        at = pl.ds(q * rows, rows)
+        part_copy(q).wait()
+        shrunk = (part[q] + got_part[q]).astype(jnp.bfloat16)
+        for side in range(2):
+            to = pl.ds(side * uhalf, uhalf)
+            up = picked(q, side, CHUNKS - 1)[:, wide - uhalf:]
+            delta = jnp.dot(shrunk, up, preferred_element_type=jnp.float32).astype(jnp.bfloat16)
+            total = own_base[at, to] + got_base[at, to] + delta.astype(jnp.float32)
+            out_ref[at, to] = total.astype(jnp.bfloat16)
+
+    for chunk in range(CHUNKS):
+        for step in range(PLANES - 1):
+            for way in range(2):
+                @pl.when(z_can(way, step))
+                def _():
+                    z_copy(way, step, chunk).wait_send()
+        for block in range(PLANES):
+            for relation in range(3):
+                p_copy(block, relation, chunk).wait_send()
+
+
+def fused(tokens, req_adapter, value_weight, adapter_down, adapter_up):
+    tok_count, width = tokens.shape
+    requests = req_adapter.shape[0]
+    adapters, rank, _ = adapter_down.shape
+    cols = adapter_up.shape[2]
+    wide = (width + cols) // 2 // CHUNKS
+    rows = tok_count // requests
+    full = PLANES * 2 * rank
+    anywhere = pl.BlockSpec(memory_space=pl.ANY)
+    dma = pltpu.SemaphoreType.DMA
+    return pl.pallas_call(
+        kernel,
+        out_shape=jax.ShapeDtypeStruct((tok_count, cols), jnp.bfloat16),
+        in_specs=[pl.BlockSpec(memory_space=pltpu.SMEM)] + [anywhere] * 4,
+        out_specs=pl.BlockSpec(memory_space=pltpu.VMEM),
+        scratch_shapes=[
+            pltpu.VMEM(tokens.shape, jnp.bfloat16),
+            pltpu.VMEM(value_weight.shape, jnp.bfloat16),
+            [pltpu.VMEM((adapters, rank, wide), jnp.bfloat16)] * (CHUNKS * (2 * PLANES - 1)),
+            pltpu.VMEM((CHUNKS, PLANES, 3, requests, rank, wide), jnp.bfloat16),
+            pltpu.VMEM((CHUNKS, requests, 2, PLANES, 2, rank, wide), jnp.bfloat16),
+            pltpu.VMEM((4, 8, 128), jnp.int32),
+            pltpu.SMEM((3, 8, 128), jnp.int32),
+            pltpu.VMEM((tok_count, cols), jnp.float32),
+            pltpu.VMEM((tok_count, cols), jnp.float32),
+            pltpu.VMEM((tok_count, cols), jnp.float32),
+            pltpu.VMEM((requests, rows, full), jnp.float32),
+            pltpu.VMEM((requests, rows, full), jnp.float32),
+            dma((2,)),
+            dma((CHUNKS, 2)),
+            dma((3,)),
+            dma((2, PLANES - 1, CHUNKS)),
+            dma((2, PLANES - 1, CHUNKS)),
+            dma((CHUNKS, PLANES, 3)),
+            dma((CHUNKS, PLANES, 3)),
+            dma((3,)),
+            dma((3,)),
+            dma,
+            dma,
+            dma((requests,)),
+            dma((requests,)),
+        ],
+        compiler_params=pltpu.CompilerParams(
+            collective_id=0, has_side_effects=True, vmem_limit_bytes=56 * 2**20
+        ),
+        cost_estimate=pl.CostEstimate(
+            flops=2 * tok_count * width * (2 * cols + full),
+            bytes_accessed=2 * (tok_count * width + width * 2 * cols),
+            transcendentals=0,
+        ),
+    )(req_adapter, tokens, value_weight, adapter_down, adapter_up)
+
+
 def solution(mesh):
     in_specs = (
         P(("groups", "dp"), "narrow"),
@@ -31,6 +334,8 @@
         P(None, "dp", "narrow"),
     )
     out_specs = P(("groups", "dp"), "narrow")
+    small = mesh.shape["groups"] == 2 and mesh.shape["dp"] == 2 * PLANES
     return jax.shard_map(
-        per_device, mesh=mesh, in_specs=in_specs, out_specs=out_specs, check_vma=False
+        fused if small else gathered,
+        mesh=mesh, in_specs=in_specs, out_specs=out_specs, check_vma=False,
     )

time: 204 us -> 59.2 us (0.29)
  waiting for transfers between devices: 157 us -> 0 us
  Pallas kernels: 0 us -> 56.9 us
  matrix products: 18.3 us -> 0 us
  between operations: 14.9 us -> 0.01 us
  blocking collectives: 4.69 us -> 0 us
  local copies, waits for them, and re-layouts: 6.55 us -> 2.06 us
  other arithmetic: 2.56 us -> 0 us
    all_gather x2 -> x0, waiting for transfers between devices: 156 us -> none  [the longest x1 124 us: per_device(): lax.all_gather(adapter_down, 'dp', axis=1, tiled=True)]
    pallas_call x0 -> x1, Pallas kernels: none -> 56.9 us  [fused(): pl.pallas_call(kernel, out_shape=jax.ShapeDtypeStruct((tok_count, cols),...]
    dot_general x3 -> x0, matrix products: 18.3 us -> none  [the longest x1 12.1 us: per_device(): jnp.dot(tokens, value_weight, preferred_element_type=jnp.float32)]
    gather x2 -> x0, local copies, waits for them, and re-layouts: 5.92 us -> none  [the longest x1 4.13 us: per_device(): jnp.take(lax.all_gather(adapter_down, 'dp', axis=1, tiled=True), req_adap...]
    psum x1 -> x0, blocking collectives: 4.69 us -> none  [per_device(): shrunk = lax.psum(result, 'narrow').astype(jnp.bfloat16)]
    convert_element_type x1 -> x0, other arithmetic: 2.54 us -> none  [per_device(): return (base + delta.astype(jnp.float32)).astype(jnp.bfloat16)]
  transfers between devices with their start and end apart: 3 -> 0, of which waited for: 2 -> 0; matrix products, arithmetic and copies ran while one was open for 12% -> 0% of each run, Pallas kernels for 0% -> 0%
where the time goes in v1:
time: 59.2 us; the launch traced here: 59 us
  Pallas kernels  56.9 us (96%)
  local copies, waits for them, and re-layouts  2.06 us (3%)
    pallas_call x1, Pallas kernels, fused(): pl.pallas_call(kernel, out_shape=jax.ShapeDtypeStruct((tok_count, cols),...  56.9 us
    unnamed x1, local copies, waits for them, and re-layouts  2.06 us

profile of v1, /device:TPU:0, one launch (start us, length us, event | category | flops | bytes accessed | tf_op | source)
XLA Modules:
  0.0 59.0 jit_solution(1196312578507275607)
XLA Ops:
  0.0 56.9 %shard_map.55 = bf16[768,512]{1,0:T(8,128)(2,1)} custom-call(s32[6]{0:T(128)} %req_ref.1, bf16[768,4096]{1,0:T(8,128)(2,1)} %tok_hbm.1, bf16[4096,1024]{1,0:T(8,128)(2,1)} %w_hbm.1, bf16[16,8,4096]{2,1,0:T(8,128)(2,1)} %down_hbm.1, bf16[16,8,512]{2,1,0:T(8,128)(2,1)} %up_hbm.1), custom_call_target="tpu_custom_call" | custom-call | flops 6845104128 | bytes 14680064 | tf_op jit(solution)/shard_map/pallas_call | solution.py:285
  56.9 2.1 %copy.7 = bf16[768,512]{1,0:T(8,128)(2,1)} copy(bf16[768,512]{1,0:T(8,128)(2,1)} %shard_map.55) | data formatting | bytes 1572864

commit v2 on v1

--- a/solution.py
+++ b/solution.py
@@ -7,7 +7,7 @@
 
 MESH = pl.DeviceIdType.MESH
 PLANES = 4
-CHUNKS = 2
+CHUNKS = 3
 TILE = 256
 
 
@@ -52,6 +52,18 @@
     yflip = d + 1 - 2 * y
     around = ((1 - g, d, c), (g, yflip, c), (1 - g, yflip, c))
     other = (g, d, 1 - c)
+
+    barrier = pltpu.get_barrier_semaphore()
+    for target in around + (other,):
+        pl.semaphore_signal(barrier, inc=1, device_id=target, device_id_type=MESH)
+
+    @pl.when(z < PLANES - 1)
+    def _():
+        pl.semaphore_signal(barrier, inc=1, device_id=above, device_id_type=MESH)
+
+    @pl.when(z > 0)
+    def _():
+        pl.semaphore_signal(barrier, inc=1, device_id=below, device_id_type=MESH)
 
     zloads = []
     for chunk in range(CHUNKS):
@@ -72,26 +84,12 @@
             zloads.append((chunk, copy))
     tok_load = pltpu.make_async_copy(tok_hbm, tok, load_sem.at[0])
     w_load = pltpu.make_async_copy(w_hbm, w, load_sem.at[1])
-    tok_load.start()
-    w_load.start()
 
     lane = lax.broadcasted_iota(jnp.int32, ids_v.shape[1:], 1)
     ids = jnp.zeros(ids_v.shape[1:], jnp.int32)
     for q in range(requests):
         ids = jnp.where(lane == q, req_ref[q], ids)
     ids_v[3] = ids
-
-    barrier = pltpu.get_barrier_semaphore()
-    for target in around + (other,):
-        pl.semaphore_signal(barrier, inc=1, device_id=target, device_id_type=MESH)
-
-    @pl.when(z < PLANES - 1)
-    def _():
-        pl.semaphore_signal(barrier, inc=1, device_id=above, device_id_type=MESH)
-
-    @pl.when(z > 0)
-    def _():
-        pl.semaphore_signal(barrier, inc=1, device_id=below, device_id_type=MESH)
 
     pl.semaphore_wait(barrier, 4 + (z + PLANES - 1) // PLANES + (2 * PLANES - 2 - z) // PLANES)
 
@@ -148,8 +146,6 @@
             device_id=around[relation], device_id_type=MESH,
         )
 
-    for relation in range(3):
-        id_copy(relation).start()
     for chunk in range(CHUNKS):
         for which, copy in zloads:
             if which == chunk:
@@ -158,6 +154,12 @@
             @pl.when(z_can(way, 0))
             def _():
                 z_copy(way, 0, chunk).start()
+
+        if chunk == 0:
+            for relation in range(3):
+                id_copy(relation).start()
+    tok_load.start()
+    w_load.start()
 
     for relation in range(3):
         id_copy(relation).wait()
@@ -206,48 +208,54 @@
             def _():
                 share(way, step, chunk)
 
-    base((1 - c) * cols, peer_base, 0, tiles)
+    base((1 - c) * cols, peer_base, 0, tiles // 2)
+    pass_on(0, 0)
+    base((1 - c) * cols, peer_base, tiles // 2, tiles)
     base_copy.start()
-    pass_on(0, 0)
+    pass_on(0, 1)
     base(c * cols, own_base, 0, tiles // 2)
-    pass_on(0, 1)
+    for chunk in range(2, CHUNKS):
+        pass_on(0, chunk)
     base(c * cols, own_base, tiles // 2, tiles)
-    for step in range(1, PLANES - 1):
-        for chunk in range(CHUNKS):
-            pass_on(step, chunk)
-
-    for chunk in range(CHUNKS):
+    for chunk in range(CHUNKS):
+        pass_on(1, chunk)
+
+    full = PLANES * 2 * rank
+
+    def picked(q, side, chunk):
+        rows8 = recv[chunk, q, side].astype(jnp.float32)
+        return rows8.reshape(full, wide).astype(jnp.bfloat16)
+
+    def part_copy(q):
+        return pltpu.make_async_remote_copy(
+            src_ref=part.at[q], dst_ref=got_part.at[q],
+            send_sem=part_send.at[q], recv_sem=part_recv.at[q],
+            device_id=other, device_id_type=MESH,
+        )
+
+    def shrink(chunk):
         for block in range(PLANES):
             for relation in range(3):
                 p_arrival(block, relation, chunk).wait_recv()
-
-    full = PLANES * 2 * rank
-
-    def picked(q, side, chunk):
-        rows8 = recv[chunk, q, side].astype(jnp.float32)
-        return rows8.reshape(full, wide).astype(jnp.bfloat16)
-
-    def part_copy(q):
-        return pltpu.make_async_remote_copy(
-            src_ref=part.at[q], dst_ref=got_part.at[q],
-            send_sem=part_send.at[q], recv_sem=part_recv.at[q],
-            device_id=other, device_id_type=MESH,
-        )
-
-    for q in range(requests):
-        at = pl.ds(q * rows, rows)
-        total = jnp.zeros((rows, full), jnp.float32)
-        for side in range(2):
-            for chunk in range(CHUNKS):
-                low = chunk * wide
-                size = min(low + wide, dhalf) - low
-                if size > 0:
-                    total += lax.dot_general(
-                        tok[at, pl.ds(side * dhalf + low, size)], picked(q, side, chunk)[:, :size],
-                        (((1,), (1,)), ((), ())), preferred_element_type=jnp.float32,
-                    )
-        part[q] = total
-        part_copy(q).start()
+        low = chunk * wide
+        size = min(low + wide, dhalf) - low
+        for q in range(requests):
+            at = pl.ds(q * rows, rows)
+            total = jnp.zeros((rows, full), jnp.float32) if chunk == 0 else part[q]
+            for side in range(2):
+                total += lax.dot_general(
+                    tok[at, pl.ds(side * dhalf + low, size)], picked(q, side, chunk)[:, :size],
+                    (((1,), (1,)), ((), ())), preferred_element_type=jnp.float32,
+                )
+            part[q] = total
+            if chunk == CHUNKS - 1:
+                part_copy(q).start()
+
+    for chunk in range(CHUNKS):
+        pass_on(2, chunk)
+        if chunk > 0:
+            shrink(chunk - 1)
+    shrink(CHUNKS - 1)
 
     base_copy.wait()
     for q in range(requests):

time: 59.2 us -> 55.6 us (0.939)
  Pallas kernels: 56.9 us -> 53.4 us
    pallas_call x1, Pallas kernels: 56.9 us -> 53.4 us  [fused(): pl.pallas_call(kernel, out_shape=jax.ShapeDtypeStruct((tok_count, cols),...]
where the time goes in v2:
time: 55.6 us; the launch traced here: 55.4 us
  Pallas kernels  53.4 us (96%)
  local copies, waits for them, and re-layouts  2.06 us (4%)
    pallas_call x1, Pallas kernels, fused(): pl.pallas_call(kernel, out_shape=jax.ShapeDtypeStruct((tok_count, cols),...  53.4 us
    unnamed x1, local copies, waits for them, and re-layouts  2.06 us

profile of v2, /device:TPU:0, one launch (start us, length us, event | category | flops | bytes accessed | tf_op | source)
XLA Modules:
  0.0 55.4 jit_solution(3175503011387126821)
XLA Ops:
  0.0 53.4 %shard_map.55 = bf16[768,512]{1,0:T(8,128)(2,1)} custom-call(s32[6]{0:T(128)} %req_ref.1, bf16[768,4096]{1,0:T(8,128)(2,1)} %tok_hbm.1, bf16[4096,1024]{1,0:T(8,128)(2,1)} %w_hbm.1, bf16[16,8,4096]{2,1,0:T(8,128)(2,1)} %down_hbm.1, bf16[16,8,512]{2,1,0:T(8,128)(2,1)} %up_hbm.1), custom_call_target="tpu_custom_call" | custom-call | flops 6845104128 | bytes 14680064 | tf_op jit(solution)/shard_map/pallas_call | solution.py:293
  53.4 2.1 %copy.7 = bf16[768,512]{1,0:T(8,128)(2,1)} copy(bf16[768,512]{1,0:T(8,128)(2,1)} %shard_map.55) | data formatting | bytes 1572864

commit v3 on v2

--- a/solution.py
+++ b/solution.py
@@ -163,9 +163,9 @@
 
     for relation in range(3):
         id_copy(relation).wait()
-        id_load = pltpu.make_async_copy(ids_v.at[relation], ids_s.at[relation], idload_sem.at[relation])
-        id_load.start()
-        id_load.wait()
+    id_load = pltpu.make_async_copy(ids_v.at[pl.ds(0, 3)], ids_s, idload_sem.at[0])
+    id_load.start()
+    id_load.wait()
     for chunk in range(CHUNKS):
         share(0, -1, chunk)
 

time: 55.6 us -> 55.6 us (level)
  no operation moved by 1% of the time
where the time goes in v3:
time: 55.6 us; the launch traced here: 55.4 us
  Pallas kernels  53.4 us (96%)
  local copies, waits for them, and re-layouts  2.06 us (4%)
    pallas_call x1, Pallas kernels, fused(): pl.pallas_call(kernel, out_shape=jax.ShapeDtypeStruct((tok_count, cols),...  53.4 us
    unnamed x1, local copies, waits for them, and re-layouts  2.06 us

profile of v3, /device:TPU:0, one launch (start us, length us, event | category | flops | bytes accessed | tf_op | source)
XLA Modules:
  0.0 55.4 jit_solution(14454048844160701141)
XLA Ops:
  0.0 53.4 %shard_map.55 = bf16[768,512]{1,0:T(8,128)(2,1)} custom-call(s32[6]{0:T(128)} %req_ref.1, bf16[768,4096]{1,0:T(8,128)(2,1)} %tok_hbm.1, bf16[4096,1024]{1,0:T(8,128)(2,1)} %w_hbm.1, bf16[16,8,4096]{2,1,0:T(8,128)(2,1)} %down_hbm.1, bf16[16,8,512]{2,1,0:T(8,128)(2,1)} %up_hbm.1), custom_call_target="tpu_custom_call" | custom-call | flops 6845104128 | bytes 14680064 | tf_op jit(solution)/shard_map/pallas_call | solution.py:293
  53.4 2.1 %copy.7 = bf16[768,512]{1,0:T(8,128)(2,1)} copy(bf16[768,512]{1,0:T(8,128)(2,1)} %shard_map.55) | data formatting | bytes 1572864
